TPU v7x, 256 devices: a whole 4x4x8 slice. The times are simulated.
256 devices in a mesh: wide: 32 (over y, z_hi, core), narrow: 8 (over x, z_lo).
Axes of the slice: x: 4, y: 4, z: 8 (z_hi: 4, z_lo: 2; z = z_hi * 2 + z_lo), core: 2. Of those that a mesh axis runs over, the one named last changes fastest.
Arguments:
- a_hamiltonian: bfloat16 [8, 32, 72, 9216], P('narrow', 'wide'), may hold values from -0.875 to 0.875
- a_margin: bfloat16 [8, 32, 72, 9216], P('narrow', 'wide'), may hold values from -0.625 to 0.625
- a_slots: int32 [8, 32, 2, 72], P('narrow', 'wide'), may hold values from 0 to 11, as said below
- a_count: int32 [8, 32], P('narrow', 'wide'), may hold values from 36 to 72, as said below
- a_molecules: int32 [8, 32, 2, 12, 16], P('narrow', 'wide'), may hold values from 0 to 393215
- b_hamiltonian: bfloat16 [8, 32, 72, 9216], P('narrow', 'wide'), may hold values from -0.875 to 0.875
- b_margin: bfloat16 [8, 32, 72, 9216], P('narrow', 'wide'), may hold values from -0.625 to 0.625
- b_slots: int32 [8, 32, 2, 72], P('narrow', 'wide'), may hold values from 0 to 11, as said below
- b_count: int32 [8, 32], P('narrow', 'wide'), may hold values from 36 to 72, as said below
- b_molecules: int32 [8, 32, 2, 12, 16], P('narrow', 'wide'), may hold values from 0 to 393215
- charge_shift: float32 [3, 393216], P(None, 'wide'), may hold values from -6 to 6
Outputs:
- product_tile: bfloat16 [8, 32, 1152, 1152], P('narrow', 'wide')
Inputs may be any that keep to these rules, and one draw needn't show every extreme that they name: `a_slots`: entries are block numbers within a tile; the first a_count entries of a tile name distinct (row, column) pairs. `a_count`: some tile has all 72 slots occupied. `b_slots`: entries are block numbers within a tile; the first b_count entries of a tile name distinct (row, column) pairs. `b_count`: some tile has all 72 slots occupied.
All inputs are finite; a program needn't handle non-finite values.
Results may differ from a plain program's by a relative error of at most 0.0057.
Values may be sent and summed in bfloat16 or wider, within the bound.
A program may use at most 128 MiB of HBM per device.

v0:
```python
import functools

import jax
import jax.numpy as jnp
from jax import lax
from jax.experimental import pallas as pl
from jax.experimental.pallas import tpu as pltpu
from jax.sharding import PartitionSpec as P

TB = 12
MB = 16
BLK = 96
SLOTS = 72
FLAT = BLK * BLK
ROWS = 16
CHUNKS = BLK // ROWS
LANES = ROWS * BLK
PART = TB * ROWS
KPAD = TB * 128
SIDE = TB * BLK
CHIPS = 16
NW, NN = 32, 8
TABLE = 12288
HALF = TABLE // 128
RAW = 1
STRIPS = RAW * LANES // 128
EARLY = 6
RELAY = 2
PIECE = 8 * BLK
CHEM = 0.3

MESH = pl.DeviceIdType.MESH
F32, BF16, I32 = jnp.float32, jnp.bfloat16, jnp.int32


def iota(shape, dim):
    return lax.broadcasted_iota(I32, shape, dim)


def kernel(
    a_h, a_m, a_slots, a_count, a_mol, b_h, b_m, b_slots, b_count, b_mol, table, out,
    h_l, m_l, h_r, m_r, blk_l, blk_r, got_l, got_r, raw_h, raw_m, hop, charge_own, charge_got, right, first, rows_ir, rows_ri,
    sel, perm, pos, pos_got, ask, asked, reply, answer, summed, lines, parts, row_q, col_q,
    load_sem, ask_s, ask_r, rep_s, rep_r, pos_s, pos_r, tab_s, tab_r,
    l_s, l_r, r_s, r_r, raw_s, raw_r, chg_s, chg_r, hop_s, hop_r, leg_s, leg_r,
):
    n, w = lax.axis_index("narrow"), lax.axis_index("wide")
    core, chip = lax.rem(w, 2), lax.div(w, 2)
    partner = w + 1 - 2 * core
    beyond = lax.rem(w - 1 + 2 * core + NW, NW)
    w_down = lax.rem(w + NW - 1, NW)
    n_down, n_up = lax.rem(n + NN - 1, NN), lax.rem(n + 1, NN)

    def dev(nn, ww):
        return {"narrow": nn, "wide": ww}

    z = 2 * lax.rem(chip, 4) + lax.rem(n, 2)

    def along_z(up):
        to = lax.rem(z + up, 8)
        return n - lax.rem(n, 2) + lax.rem(to, 2), 2 * (chip - lax.rem(chip, 4) + lax.div(to, 2))

    up_n, up_w = along_z(3)
    from_n, from_w = along_z(5)
    relay = dev(up_n, up_w)
    last = dev(from_n, lax.rem(from_w + NW - 1, NW))
    home = lax.rem(chip + 1, CHIPS)
    zr = lax.rem(2 * lax.rem(home, 4) + lax.rem(n, 2) + 3, 8)
    giver = dev(n - lax.rem(n, 2) + lax.rem(zr, 2), 2 * (home - lax.rem(home, 4) + lax.div(zr, 2)))

    chip_y, chip_z = lax.div(chip, 4), lax.rem(chip, 4)

    def peer(k):
        return dev(n, 8 * lax.rem(chip_y + k // 4, 4) + 2 * lax.rem(chip_z + k % 4, 4) + core)

    def back(k):
        return (4 - k // 4) % 4 * 4 + (4 - k % 4) % 4

    loads = [
        pltpu.make_async_copy(src, dst, load_sem.at[k])
        for k, (src, dst) in enumerate([(b_h, h_r), (b_m, m_r), (a_h, h_l), (a_m, m_l)])
    ]
    for copy in loads:
        copy.start()

    barrier = pltpu.get_barrier_semaphore()
    known = [peer(i) for i in range(1, CHIPS)]
    known += [dev(n, partner), dev(n, beyond), dev(n_down, w), dev(n_up, w)]
    for device in known:
        pl.semaphore_signal(barrier, inc=1, device_id=device, device_id_type=MESH)

    @pl.when(core == 0)
    def _():
        for device in (relay, dev(from_n, from_w), last):
            pl.semaphore_signal(barrier, inc=1, device_id=device, device_id_type=MESH)

    @pl.when(core == 1)
    def _():
        pl.semaphore_signal(barrier, inc=1, device_id=giver, device_id_type=MESH)

    mols = jnp.concatenate([a_mol[:, 0, :], a_mol[:, 1, :], b_mol[:, 0, :], b_mol[:, 1, :]], axis=1)
    folded = jnp.concatenate([mols[0:6], mols[6:12]], axis=1)
    ask[0:6, :] = folded
    ask[6:8, :] = jnp.zeros((2, 128), I32)
    asked[0, 0:6, :] = folded
    for f, (slots, count) in enumerate([(a_slots, a_count), (b_slots, b_count)]):
        place = slots[1:2, :] * (2 * TB) + slots[0:1, :]
        live = iota((1, SLOTS), 1) < count[0:1, 0:1]
        pos[f] = jnp.full((8, 128), -1, I32)
        pos[f, 0:1, 0:SLOTS] = jnp.where(live, place, -1)
        pos[f, 1:3, 0:SLOTS] = slots[...]

    def line(h, _):
        for q in range(3):
            lines[q, pl.ds(h, 1), :] = table[q : q + 1, pl.ds(pl.multiple_of(h * 128, 128), 128)]
        return 0

    lax.fori_loop(0, HALF, line, 0, unroll=8)
    for q in range(3):
        top = lines[q].astype(BF16)
        parts[q * HALF : (q + 1) * HALF, 0:128] = top
        parts[q * HALF : (q + 1) * HALF, 128:256] = (lines[q] - top.astype(F32)).astype(BF16)

    pl.semaphore_wait(barrier, len(known) + 3 - 2 * core)

    def remote(src, dst, s, r, device):
        return pltpu.make_async_remote_copy(
            src_ref=src, dst_ref=dst, send_sem=s, recv_sem=r, device_id=device, device_id_type=MESH
        )

    asks = [remote(ask, asked.at[back(i)], ask_s.at[i], ask_r.at[back(i)], peer(i)) for i in range(1, CHIPS)]
    for copy in asks:
        copy.start()
    tab_copy = remote(
        parts.at[0 : 3 * HALF], parts.at[3 * HALF : 6 * HALF], tab_s, tab_r, dev(n, partner)
    )
    tab_copy.start()
    pos_copies = [
        remote(pos.at[0], pos_got.at[0], pos_s.at[0], pos_r.at[0], dev(n, w_down)),
        remote(pos.at[1], pos_got.at[1], pos_s.at[1], pos_r.at[1], dev(n_down, w)),
    ]
    for copy in pos_copies:
        copy.start()

    def chunk_lanes(c):
        return pl.ds(pl.multiple_of(c * LANES, 128), LANES)

    def strip(k):
        at = pl.ds(pl.multiple_of(k * 128, 128), 128)
        remote(b_h.at[:, at], raw_h.at[:, at], raw_s.at[0], raw_r.at[0], dev(n_down, w)).start()
        remote(b_m.at[:, at], raw_m.at[:, at], raw_s.at[1], raw_r.at[1], dev(n_down, w)).start()

    strips = slice(0, RAW * LANES)
    raws = [
        remote(b_h.at[:, strips], raw_h, raw_s.at[0], raw_r.at[0], dev(n_down, w)),
        remote(b_m.at[:, strips], raw_m, raw_s.at[1], raw_r.at[1], dev(n_down, w)),
    ]
    for k in range(EARLY):
        strip(k)

    def selection(k, place):
        wide = jnp.concatenate([place, jnp.where(place < 0, -1, place + TB)], axis=1)
        hit = iota((2 * TB * TB, 2 * SLOTS), 0) == wide
        sel[k] = jnp.where(hit, 1.0, 0.0).astype(BF16)

    selection(0, pos[0, 0:1, 0:SLOTS])
    selection(1, pos[1, 0:1, 0:SLOTS])
    pr, pc = iota((PART, PART), 0), iota((PART, PART), 1)
    perm[...] = jnp.where(pc == (pr % ROWS) * TB + pr // ROWS, 1.0, 0.0).astype(BF16)
    for k in range(2):
        for t in range(TB):
            right[k, t * 128 + BLK : (t + 1) * 128, :] = jnp.zeros((128 - BLK, SIDE), BF16)

    tab_copy.wait_recv()
    low = iota((128, 256), 0)
    high = iota((HALF, 256), 0)

    def search(k):
        ids = asked[k, 0:6, :] - chip * (2 * TABLE)
        for j in range(0, 6, 2):
            mine = jnp.concatenate([ids[j : j + 1], ids[j + 1 : j + 2]], axis=1)
            hi, lo = mine >> 7, mine & 127
            one = jnp.where(low == lo, 1.0, 0.0).astype(BF16)
            one = jnp.concatenate([one, one], axis=0)
            both = jnp.dot(parts[...], one, preferred_element_type=F32)
            in_own, in_other = high == hi - core * HALF, high == hi - (1 - core) * HALF
            for q in range(3):
                own = both[q * HALF : (q + 1) * HALF]
                other = both[(q + 3) * HALF : (q + 4) * HALF]
                hit = jnp.where(in_own, own, jnp.where(in_other, other, 0.0))
                hit = jnp.sum(hit, axis=0, keepdims=True)
                reply[k, 6 * q + j : 6 * q + j + 1, :] = hit[:, 0:128]
                reply[k, 6 * q + j + 1 : 6 * q + j + 2, :] = hit[:, 128:256]

    def serve(k, _):
        remote(ask, asked.at[k], ask_s.at[k], ask_r.at[k], peer(k)).wait_recv()
        search(k)

        @pl.when(k < 4 + STRIPS - EARLY)
        def _():
            strip(k + EARLY - 4)

        return 0

    y_copies = []
    search(0)
    for dy in range(1, 4):
        lax.fori_loop(4 * dy, 4 * dy + 4, serve, 0)
        y_copies.append(
            remote(reply.at[pl.ds(4 * dy, 4)], answer.at[4 - dy], rep_s.at[dy], rep_r.at[4 - dy], peer(4 * dy))
        )
        y_copies[-1].start()
    for k in range(1, 4):
        remote(ask, asked.at[k], ask_s.at[k], ask_r.at[k], peer(k)).wait_recv()
        search(k)
    for copy in y_copies:
        copy.wait_recv()
    for k in range(4):
        reply[k] = reply[k] + answer[1, k] + answer[2, k] + answer[3, k]
    z_copies = [
        remote(reply.at[dz], summed.at[4 - dz], rep_s.at[3 + dz], rep_r.at[7 - dz], peer(dz)) for dz in range(1, 4)
    ]
    for copy in z_copies:
        copy.start()
    for copy in z_copies:
        copy.wait_recv()
    replies = y_copies + z_copies
    total = reply[0] + summed[1] + summed[2] + summed[3]
    charge_own[...] = total
    charge_copy = remote(charge_own, charge_got, chg_s, chg_r, dev(n_down, w))
    charge_copy.start()

    lane = iota((16, 128), 1)

    def orbitals(charges, side, flat):
        i = flat % BLK
        mol, a = i // 6, i % 6
        got = []
        for q in range(3):
            part = charges[6 * q : 6 * q + 6, :]
            part = jnp.concatenate([part, pltpu.roll(part, 64, 1), jnp.zeros((4, 128), F32)], axis=0)
            got.append(jnp.take_along_axis(part, mol + MB * side, axis=1))
        return jnp.where(a < 4, got[0], jnp.where(a == 4, got[1], got[2]))

    def pick(place, values):
        one = jnp.where(iota((16, SLOTS), 0) == place, 1.0, 0.0)
        return lax.dot_general(
            one, values, (((0,), (0,)), ((), ())), precision=lax.Precision.HIGHEST, preferred_element_type=F32
        )

    def shifts(f, charges, side, row, col):
        row_q[f] = pick(row, orbitals(charges, side, lane))
        for p in range(3):
            col_q[f, p] = pick(col, orbitals(charges, side + 1, lane + 128 * p))

    shifts(1, total, 2, b_slots[0:1, :], b_slots[1:2, :])

    wide_lane = iota((SLOTS, 128), 1)

    def assemble(f, h_ref, m_ref, blk):
        def group(g, _):
            for p in range(3):
                lanes = pl.ds(pl.multiple_of((3 * g + p) * 128, 128), 128)
                h, m = h_ref[:, lanes].astype(F32), m_ref[:, lanes].astype(F32)
                i = 4 * g + (wide_lane + 128 * p) // BLK
                shift = jnp.take_along_axis(row_q[f], i, axis=1) + col_q[f, p]
                hamiltonian = h + 0.5 * m * shift
                blk[:, lanes] = (CHEM * m - hamiltonian).astype(BF16)
            return 0

        return group

    def send_r(c):
        at = chunk_lanes(c)
        return remote(blk_r.at[:, at], got_r.at[:, at], r_s.at[c], r_r.at[c], dev(n_down, w))

    def send_l(c):
        at = chunk_lanes(c)
        return remote(blk_l.at[:, at], got_l.at[:, at], l_s.at[c], l_r.at[c], dev(n, w_down))

    def piece(k):
        return slice(k * PIECE, (k + 1) * PIECE)

    def first_leg(k):
        return remote(blk_l.at[:, piece(k)], hop.at[:, piece(k)], hop_s.at[k], hop_r.at[k], relay)

    def second_leg(k):
        return remote(hop.at[:, piece(k)], got_l.at[:, piece(k)], leg_s.at[k], leg_r.at[k], last)

    def straight(k):
        return remote(blk_l.at[:, piece(k)], got_l.at[:, piece(k)], leg_s.at[k], leg_r.at[k], dev(n, w_down))

    def make_r(c, _):
        lax.fori_loop(4 * c, 4 * c + 4, assemble(1, h_r, m_r, blk_r), 0)
        send_r(c).start()
        return 0

    for copy in loads:
        copy.wait()
    make_r(RAW, 0)
    shifts(0, total, 0, a_slots[0:1, :], a_slots[1:2, :])
    lax.fori_loop(0, 4, assemble(0, h_l, m_l, blk_l), 0)

    @pl.when(core == 0)
    def _():
        for k in range(RELAY):
            first_leg(k).start()

    @pl.when(core == 1)
    def _():
        for k in range(RELAY):
            straight(k).start()

    lax.fori_loop(RAW + 1, CHUNKS, make_r, 0)
    lax.fori_loop(0, 4 * RAW, assemble(1, h_r, m_r, blk_r), 0)
    lax.fori_loop(4, 4 * CHUNKS, assemble(0, h_l, m_l, blk_l), 0)
    send_l(1).start()

    lane72 = iota((SLOTS, 128), 1)
    lane24 = iota((2 * TB, 128), 1)

    def spread(k, blk, c, compact):
        def group(q):
            at = pl.multiple_of(c * LANES + q * 384, 128)
            t = [blk[:, pl.ds(pl.multiple_of(at + 128 * p, 128), 128)].astype(F32) for p in range(3)]
            y0 = t[0]
            y1 = pltpu.roll(jnp.where(lane72 >= 96, t[0], t[1]), 32, 1)
            y2 = pltpu.roll(jnp.where(lane72 >= 64, t[1], t[2]), 64, 1)
            y3 = pltpu.roll(t[2], 96, 1)
            pairs = jnp.concatenate(
                [jnp.concatenate([y0, y1], axis=0), jnp.concatenate([y2, y3], axis=0)], axis=1
            ).astype(BF16)
            d = jnp.dot(sel[k], pairs, preferred_element_type=F32)
            tiles = []
            for half in range(2):
                b = [d[t * 2 * TB : (t + 1) * 2 * TB, 128 * half : 128 * half + 128] for t in range(TB)]
                if compact:
                    packed = []
                    for g in range(0, TB, 4):
                        r1, r2, r3 = (pltpu.roll(b[g + 1 + s], 96 - 32 * s, 1) for s in range(3))
                        packed += [
                            jnp.where(lane24 < 96, b[g], r1),
                            jnp.where(lane24 < 64, r1, r2),
                            jnp.where(lane24 < 32, r2, r3),
                        ]
                    b = packed
                tiles.append(b)
            at = slice(q * 4 * TB, (q + 1) * 4 * TB)
            for t, (top, low) in enumerate(zip(*tiles, strict=True)):
                rows_ir[at, 128 * t : 128 * t + 128] = jnp.concatenate([top, low], axis=0).astype(BF16)

        for q in range(ROWS // 4):
            group(q)

    def spread_right(k, blk, c, dst):
        spread(k, blk, c, True)
        for s in range(3):
            at = slice(384 * s, 384 * s + 384)
            ordered = jnp.dot(perm[...], rows_ir[:, at], preferred_element_type=F32).astype(BF16)
            for t in range(TB):
                to = pl.ds(pl.multiple_of(t * 128 + c * ROWS, 16), ROWS)
                right[dst, to, at] = ordered[t * ROWS : (t + 1) * ROWS]

    def spread_left(k, blk, c):
        spread(k, blk, c, False)
        for s in range(3):
            at = slice(512 * s, 512 * s + 512)
            rows_ri[:, at] = jnp.dot(perm[...], rows_ir[:, at], preferred_element_type=F32).astype(BF16)

    def own_right(c, _):
        spread_right(1, blk_r, c, 0)
        return 0

    def own_left(c, _):
        spread_left(0, blk_l, c)
        for s in range(3):
            at = slice(384 * s, 384 * s + 384)
            first[c, :, at] = jnp.dot(rows_ri[...], right[0, :, at], preferred_element_type=F32)
        return 0

    lax.fori_loop(0, CHUNKS, own_right, 0)
    send_l(2).start()
    send_l(3).start()
    lax.fori_loop(0, CHUNKS // 2, own_left, 0)

    @pl.when(core == 0)
    def _():
        for k in range(RELAY):
            first_leg(k).wait_recv()
            second_leg(k).start()

    lax.fori_loop(CHUNKS // 2, CHUNKS, own_left, 0)

    for copy in pos_copies:
        copy.wait_recv()
    selection(2, pos_got[0, 0:1, 0:SLOTS])
    selection(3, pos_got[1, 0:1, 0:SLOTS])

    send_l(4).start()
    send_l(5).start()
    charge_copy.wait_recv()
    shifts(2, charge_got[...], 2, pos_got[1, 1:2, 0:SLOTS], pos_got[1, 2:3, 0:SLOTS])
    for copy in raws:
        copy.wait_recv()
    lax.fori_loop(0, 4 * RAW, assemble(2, raw_h, raw_m, got_r), 0)

    def next_raw(c, _):
        spread_right(3, got_r, c, 1)
        return 0

    def next_right(c, _):
        send_r(c).wait_recv()
        spread_right(3, got_r, c, 1)
        return 0

    lax.fori_loop(0, RAW, next_raw, 0)
    lax.fori_loop(RAW, CHUNKS, next_right, 0)

    def finish_left(c):
        spread_left(2, got_l, c)
        rows = pl.ds(pl.multiple_of(c * ROWS, 16), ROWS)
        for s in range(3):
            at = slice(384 * s, 384 * s + 384)
            both = first[c, :, at] + jnp.dot(rows_ri[...], right[1, :, at], preferred_element_type=F32)
            both = both.astype(BF16)
            for t in range(TB):
                out[t, rows, at] = both[t * ROWS : (t + 1) * ROWS]

    def next_left(c, _):
        send_l(c).wait_recv()
        finish_left(c)
        return 0

    for copy in asks + replies + pos_copies + raws + [tab_copy, charge_copy]:
        copy.wait_send()
    lax.fori_loop(1, 3, next_left, 0)
    for k in range(RELAY):
        straight(k).wait_recv()
    finish_left(0)
    lax.fori_loop(3, CHUNKS, next_left, 0)

    def finish(c, _):
        send_l(c).wait_send()
        return 0

    lax.fori_loop(1, CHUNKS, finish, 0)
    for k in range(RELAY):
        straight(k).wait_send()

    @pl.when(core == 0)
    def _():
        for k in range(RELAY):
            first_leg(k).wait_send()

    for c in range(RAW, CHUNKS):
        send_r(c).wait_send()


def local(*args):
    a_h, a_m, a_slots, a_count, a_mol, b_h, b_m, b_slots, b_count, b_mol, table = args
    anywhere = pl.BlockSpec(memory_space=pl.ANY)
    vmem = pl.BlockSpec(memory_space=pltpu.VMEM)
    dma = pltpu.SemaphoreType.DMA
    tile = pltpu.VMEM((SLOTS, FLAT), BF16)
    raw = pltpu.VMEM((SLOTS, RAW * LANES), BF16)
    scratch = [tile] * 8 + [raw] * 2 + [
        pltpu.VMEM((SLOTS, RELAY * PIECE), BF16),
        pltpu.VMEM((18, 128), F32),
        pltpu.VMEM((18, 128), F32),
        pltpu.VMEM((2, KPAD, SIDE), BF16),
        pltpu.VMEM((CHUNKS, PART, SIDE), F32),
        pltpu.VMEM((PART, KPAD), BF16),
        pltpu.VMEM((PART, KPAD), BF16),
        pltpu.VMEM((4, 2 * TB * TB, 2 * SLOTS), BF16),
        pltpu.VMEM((PART, PART), BF16),
        pltpu.VMEM((2, 8, 128), I32),
        pltpu.VMEM((2, 8, 128), I32),
        pltpu.VMEM((8, 128), I32),
        pltpu.VMEM((CHIPS, 8, 128), I32),
        pltpu.VMEM((CHIPS, 18, 128), F32),
        pltpu.VMEM((4, 4, 18, 128), F32),
        pltpu.VMEM((4, 18, 128), F32),
        pltpu.VMEM((3, HALF, 128), F32),
        pltpu.VMEM((6 * HALF, 256), BF16),
        pltpu.VMEM((3, SLOTS, 128), F32),
        pltpu.VMEM((3, 3, SLOTS, 128), F32),
        dma((4,)),
        dma((CHIPS,)), dma((CHIPS,)), dma((CHIPS,)), dma((CHIPS,)),
        dma((2,)), dma((2,)), dma(()), dma(()),
        dma((CHUNKS,)), dma((CHUNKS,)), dma((CHUNKS,)), dma((CHUNKS,)),
        dma((2,)), dma((2,)), dma(()), dma(()),
        dma((RELAY,)), dma((RELAY,)), dma((4,)), dma((4,)),
    ]
    result = pl.pallas_call(
        kernel,
        out_shape=pltpu.VMEM((TB, BLK, SIDE), BF16),
        in_specs=[anywhere, anywhere, vmem, vmem, vmem, anywhere, anywhere, vmem, vmem, vmem, vmem],
        out_specs=vmem,
        scratch_shapes=scratch,
        compiler_params=pltpu.CompilerParams(
            collective_id=0, has_side_effects=True, vmem_limit_bytes=56 * 2**20
        ),
        cost_estimate=pl.CostEstimate(flops=14 * 10**9, bytes_accessed=9 * 10**6, transcendentals=0),
    )(
        a_h[0, 0], a_m[0, 0], a_slots[0, 0], a_count, jnp.swapaxes(a_mol[0, 0], 0, 1),
        b_h[0, 0], b_m[0, 0], b_slots[0, 0], b_count, jnp.swapaxes(b_mol[0, 0], 0, 1), table,
    )
    return result.reshape(1, 1, SIDE, SIDE)


def solution(mesh):
    blocks = P("narrow", "wide", None, None)
    count = P("narrow", "wide")
    molecules = P("narrow", "wide", None, None, None)
    factor = (blocks, blocks, blocks, count, molecules)
    return jax.shard_map(
        local,
        mesh=mesh,
        in_specs=factor + factor + (P(None, "wide"),),
        out_specs=blocks,
        check_vma=False,
    )
```

profile of v0, /device:TPU:53, one launch (start us, length us, event | category | flops | bytes accessed | tf_op | source)
XLA Modules:
  0.0 81.0 jit_solution(10407519913415673280)
XLA Ops:
  1.3 78.2 %shard_map.109 = bf16[12,96,1152]{2,1,0:T(8,128)(2,1)S(1)} custom-call(bf16[72,9216]{1,0:T(8,128)(2,1)} %bitcast.14, bf16[72,9216]{1,0:T(8,128)(2,1)} %bitcast.15, s32[2,72]{1,0:T(2,128)} %bitcast.20, s32[1,1]{1,0:T(1,128)S(6)} %copy.14.a_count, s32[12,2,16]{2,1,0:T(2,128)} %bitcast.18, bf16[72,9216]{1,0:T(8,128)(2,1)} %bitcast.16, ...), custom_call_target="tpu_custom_call" | custom-call | flops 14000000000 | bytes 9000000 | tf_op jit(solution)/shard_map/pallas_call | solution.py:494
  79.5 1.5 %copy.13 = bf16[1,1,1152,1152]{3,2,1,0:T(8,128)(2,1)} copy(bf16[1,1,1152,1152]{3,2,1,0:T(8,128)(2,1)S(1)} %bitcast.13) | data formatting | bytes 5308416
where the time goes:
time: 81.1 us; the launch traced here: 81 us
  Pallas kernels  78.2 us (96%)
  local copies, waits for them, and re-layouts  1.5 us (2%)
  between operations  1.31 us (2%)
    pallas_call x1, Pallas kernels, local(): pl.pallas_call(kernel, out_shape=pltpu.VMEM((TB, BLK, SIDE), BF16), in_sp...  78.2 us

commit v1 on v0

--- a/solution.py
+++ b/solution.py
@@ -22,9 +22,12 @@
 NW, NN = 32, 8
 TABLE = 12288
 HALF = TABLE // 128
-RAW = 1
-STRIPS = RAW * LANES // 128
-EARLY = 6
+RAW = 24
+REST = (RAW // ROWS + 1) * ROWS - RAW
+FULL = (RAW + REST) // ROWS
+STRIPS = RAW * BLK // 128
+EARLY = 8
+LATE = 4
 RELAY = 2
 PIECE = 8 * BLK
 CHEM = 0.3
@@ -150,7 +153,7 @@
         remote(b_h.at[:, at], raw_h.at[:, at], raw_s.at[0], raw_r.at[0], dev(n_down, w)).start()
         remote(b_m.at[:, at], raw_m.at[:, at], raw_s.at[1], raw_r.at[1], dev(n_down, w)).start()
 
-    strips = slice(0, RAW * LANES)
+    strips = slice(0, RAW * BLK)
     raws = [
         remote(b_h.at[:, strips], raw_h, raw_s.at[0], raw_r.at[0], dev(n_down, w)),
         remote(b_m.at[:, strips], raw_m, raw_s.at[1], raw_r.at[1], dev(n_down, w)),
@@ -173,7 +176,7 @@
 
     tab_copy.wait_recv()
     low = iota((128, 256), 0)
-    high = iota((HALF, 256), 0)
+    line8 = iota((8, 256), 0)
 
     def search(k):
         ids = asked[k, 0:6, :] - chip * (2 * TABLE)
@@ -183,12 +186,15 @@
             one = jnp.where(low == lo, 1.0, 0.0).astype(BF16)
             one = jnp.concatenate([one, one], axis=0)
             both = jnp.dot(parts[...], one, preferred_element_type=F32)
-            in_own, in_other = high == hi - core * HALF, high == hi - (1 - core) * HALF
+            hits = [jnp.zeros((8, 256), F32)] * 3
+            for side, base in ((0, core * HALF), (3, (1 - core) * HALF)):
+                for t in range(0, HALF, 8):
+                    here = line8 == hi - (base + t)
+                    for q in range(3):
+                        at = (q + side) * HALF + t
+                        hits[q] = jnp.where(here, both[at : at + 8], hits[q])
             for q in range(3):
-                own = both[q * HALF : (q + 1) * HALF]
-                other = both[(q + 3) * HALF : (q + 4) * HALF]
-                hit = jnp.where(in_own, own, jnp.where(in_other, other, 0.0))
-                hit = jnp.sum(hit, axis=0, keepdims=True)
+                hit = jnp.sum(hits[q], axis=0, keepdims=True)
                 reply[k, 6 * q + j : 6 * q + j + 1, :] = hit[:, 0:128]
                 reply[k, 6 * q + j + 1 : 6 * q + j + 2, :] = hit[:, 128:256]
 
@@ -196,7 +202,7 @@
         remote(ask, asked.at[k], ask_s.at[k], ask_r.at[k], peer(k)).wait_recv()
         search(k)
 
-        @pl.when(k < 4 + STRIPS - EARLY)
+        @pl.when(k < 4 + STRIPS - EARLY - LATE)
         def _():
             strip(k + EARLY - 4)
 
@@ -222,6 +228,8 @@
     ]
     for copy in z_copies:
         copy.start()
+    for k in range(STRIPS - LATE, STRIPS):
+        strip(k)
     for copy in z_copies:
         copy.wait_recv()
     replies = y_copies + z_copies
@@ -290,6 +298,9 @@
     def straight(k):
         return remote(blk_l.at[:, piece(k)], got_l.at[:, piece(k)], leg_s.at[k], leg_r.at[k], dev(n, w_down))
 
+    rest_at = slice(RAW * BLK, (RAW + REST) * BLK)
+    rest = remote(blk_r.at[:, rest_at], got_r.at[:, rest_at], r_s.at[0], r_r.at[0], dev(n_down, w))
+
     def make_r(c, _):
         lax.fori_loop(4 * c, 4 * c + 4, assemble(1, h_r, m_r, blk_r), 0)
         send_r(c).start()
@@ -297,7 +308,8 @@
 
     for copy in loads:
         copy.wait()
-    make_r(RAW, 0)
+    lax.fori_loop(RAW // 4, (RAW + REST) // 4, assemble(1, h_r, m_r, blk_r), 0)
+    rest.start()
     shifts(0, total, 0, a_slots[0:1, :], a_slots[1:2, :])
     lax.fori_loop(0, 4, assemble(0, h_l, m_l, blk_l), 0)
 
@@ -311,8 +323,8 @@
         for k in range(RELAY):
             straight(k).start()
 
-    lax.fori_loop(RAW + 1, CHUNKS, make_r, 0)
-    lax.fori_loop(0, 4 * RAW, assemble(1, h_r, m_r, blk_r), 0)
+    lax.fori_loop(FULL, CHUNKS, make_r, 0)
+    lax.fori_loop(0, RAW // 4, assemble(1, h_r, m_r, blk_r), 0)
     lax.fori_loop(4, 4 * CHUNKS, assemble(0, h_l, m_l, blk_l), 0)
     send_l(1).start()
 
@@ -402,7 +414,8 @@
     shifts(2, charge_got[...], 2, pos_got[1, 1:2, 0:SLOTS], pos_got[1, 2:3, 0:SLOTS])
     for copy in raws:
         copy.wait_recv()
-    lax.fori_loop(0, 4 * RAW, assemble(2, raw_h, raw_m, got_r), 0)
+    lax.fori_loop(0, RAW // 4, assemble(2, raw_h, raw_m, got_r), 0)
+    rest.wait_recv()
 
     def next_raw(c, _):
         spread_right(3, got_r, c, 1)
@@ -413,8 +426,8 @@
         spread_right(3, got_r, c, 1)
         return 0
 
-    lax.fori_loop(0, RAW, next_raw, 0)
-    lax.fori_loop(RAW, CHUNKS, next_right, 0)
+    lax.fori_loop(0, FULL, next_raw, 0)
+    lax.fori_loop(FULL, CHUNKS, next_right, 0)
 
     def finish_left(c):
         spread_left(2, got_l, c)
@@ -452,7 +465,8 @@
         for k in range(RELAY):
             first_leg(k).wait_send()
 
-    for c in range(RAW, CHUNKS):
+    rest.wait_send()
+    for c in range(FULL, CHUNKS):
         send_r(c).wait_send()
 
 
@@ -462,7 +476,7 @@
     vmem = pl.BlockSpec(memory_space=pltpu.VMEM)
     dma = pltpu.SemaphoreType.DMA
     tile = pltpu.VMEM((SLOTS, FLAT), BF16)
-    raw = pltpu.VMEM((SLOTS, RAW * LANES), BF16)
+    raw = pltpu.VMEM((SLOTS, RAW * BLK), BF16)
     scratch = [tile] * 8 + [raw] * 2 + [
         pltpu.VMEM((SLOTS, RELAY * PIECE), BF16),
         pltpu.VMEM((18, 128), F32),

time: 81.1 us -> 79.2 us (0.977)
  Pallas kernels: 78.2 us -> 75.5 us
    pallas_call x1, Pallas kernels: 78.2 us -> 75.5 us  [local(): pl.pallas_call(kernel, out_shape=pltpu.VMEM((TB, BLK, SIDE), BF16), in_sp...]
where the time goes in v1:
time: 79.2 us; the launch traced here: 78.3 us
  Pallas kernels  75.5 us (95%)
  local copies, waits for them, and re-layouts  1.5 us (2%)
  between operations  1.31 us (2%)
    pallas_call x1, Pallas kernels, local(): pl.pallas_call(kernel, out_shape=pltpu.VMEM((TB, BLK, SIDE), BF16), in_sp...  75.5 us

profile of v1, /device:TPU:53, one launch (start us, length us, event | category | flops | bytes accessed | tf_op | source)
XLA Modules:
  0.0 78.3 jit_solution(4308175985651468834)
XLA Ops:
  1.3 75.5 %shard_map.109 = bf16[12,96,1152]{2,1,0:T(8,128)(2,1)S(1)} custom-call(bf16[72,9216]{1,0:T(8,128)(2,1)} %bitcast.14, bf16[72,9216]{1,0:T(8,128)(2,1)} %bitcast.15, s32[2,72]{1,0:T(2,128)} %bitcast.20, s32[1,1]{1,0:T(1,128)S(6)} %copy.14.a_count, s32[12,2,16]{2,1,0:T(2,128)} %bitcast.18, bf16[72,9216]{1,0:T(8,128)(2,1)} %bitcast.16, ...), custom_call_target="tpu_custom_call" | custom-call | flops 14000000000 | bytes 9000000 | tf_op jit(solution)/shard_map/pallas_call | solution.py:508
  76.8 1.5 %copy.13 = bf16[1,1,1152,1152]{3,2,1,0:T(8,128)(2,1)} copy(bf16[1,1,1152,1152]{3,2,1,0:T(8,128)(2,1)S(1)} %bitcast.13) | data formatting | bytes 5308416

commit v2 on v1

--- a/solution.py
+++ b/solution.py
@@ -22,11 +22,11 @@
 NW, NN = 32, 8
 TABLE = 12288
 HALF = TABLE // 128
-RAW = 24
+RAW = 20
 REST = (RAW // ROWS + 1) * ROWS - RAW
 FULL = (RAW + REST) // ROWS
 STRIPS = RAW * BLK // 128
-EARLY = 8
+EARLY = 9
 LATE = 4
 RELAY = 2
 PIECE = 8 * BLK
@@ -101,11 +101,12 @@
     def _():
         pl.semaphore_signal(barrier, inc=1, device_id=giver, device_id_type=MESH)
 
-    mols = jnp.concatenate([a_mol[:, 0, :], a_mol[:, 1, :], b_mol[:, 0, :], b_mol[:, 1, :]], axis=1)
-    folded = jnp.concatenate([mols[0:6], mols[6:12]], axis=1)
-    ask[0:6, :] = folded
+    for at, mol in ((0, b_mol), (3, a_mol)):
+        mols = jnp.concatenate([mol[:, 0, :], mol[:, 1, :]], axis=1)
+        folded = jnp.concatenate([mols[3 * g : 3 * g + 3] for g in range(4)], axis=1)
+        ask[at : at + 3, :] = folded
+        asked[0, at : at + 3, :] = folded
     ask[6:8, :] = jnp.zeros((2, 128), I32)
-    asked[0, 0:6, :] = folded
     for f, (slots, count) in enumerate([(a_slots, a_count), (b_slots, b_count)]):
         place = slots[1:2, :] * (2 * TB) + slots[0:1, :]
         live = iota((1, SLOTS), 1) < count[0:1, 0:1]
@@ -131,7 +132,8 @@
             src_ref=src, dst_ref=dst, send_sem=s, recv_sem=r, device_id=device, device_id_type=MESH
         )
 
-    asks = [remote(ask, asked.at[back(i)], ask_s.at[i], ask_r.at[back(i)], peer(i)) for i in range(1, CHIPS)]
+    asks = [remote(ask, asked.at[back(i)], ask_s, ask_r.at[back(i)], peer(i)) for i in range(1, CHIPS)]
+    all_asks = remote(asked.at[pl.ds(1, CHIPS - 1)], asked.at[pl.ds(1, CHIPS - 1)], ask_s, ask_r.at[0], peer(1))
     for copy in asks:
         copy.start()
     tab_copy = remote(
@@ -178,8 +180,9 @@
     low = iota((128, 256), 0)
     line8 = iota((8, 256), 0)
 
-    def search(k):
-        ids = asked[k, 0:6, :] - chip * (2 * TABLE)
+    def search(half, k):
+        rows = slice(3 * half, 3 * half + 3)
+        ids = jnp.concatenate([asked[k, rows, :], asked[k + 1, rows, :]], axis=0) - chip * (2 * TABLE)
         for j in range(0, 6, 2):
             mine = jnp.concatenate([ids[j : j + 1], ids[j + 1 : j + 2]], axis=1)
             hi, lo = mine >> 7, mine & 127
@@ -195,46 +198,79 @@
                         hits[q] = jnp.where(here, both[at : at + 8], hits[q])
             for q in range(3):
                 hit = jnp.sum(hits[q], axis=0, keepdims=True)
-                reply[k, 6 * q + j : 6 * q + j + 1, :] = hit[:, 0:128]
-                reply[k, 6 * q + j + 1 : 6 * q + j + 2, :] = hit[:, 128:256]
-
-    def serve(k, _):
-        remote(ask, asked.at[k], ask_s.at[k], ask_r.at[k], peer(k)).wait_recv()
-        search(k)
-
-        @pl.when(k < 4 + STRIPS - EARLY - LATE)
+                for i in range(2):
+                    to = 3 * q + (j + i) % 3
+                    reply[half, k + (j + i) // 3, to : to + 1, :] = hit[:, 128 * i : 128 * i + 128]
+
+    def asked_by(k):
+        remote(ask, asked.at[k], ask_s, ask_r.at[k], peer(k)).wait_recv()
+
+    def serve(t, _):
+        k = 2 * t
+        asked_by(k)
+        asked_by(k + 1)
+        search(0, k)
+
+        @pl.when(t < 2 + STRIPS - EARLY - LATE)
         def _():
-            strip(k + EARLY - 4)
-
-        return 0
-
-    y_copies = []
-    search(0)
+            strip(t + EARLY - 2)
+
+        return 0
+
+    def serve_a(t, _):
+        search(1, 2 * t)
+        return 0
+
+    def send_y(half, dy):
+        copy = remote(
+            reply.at[half, pl.ds(4 * dy, 4)], answer.at[half, 4 - dy],
+            rep_s.at[7 * half + dy], rep_r.at[7 * half + 4 - dy], peer(4 * dy),
+        )
+        copy.start()
+        return copy
+
+    def send_z(half, y_copies):
+        for copy in y_copies:
+            copy.wait_recv()
+        for k in range(4):
+            reply[half, k] = reply[half, k] + answer[half, 1, k] + answer[half, 2, k] + answer[half, 3, k]
+        copies = [
+            remote(
+                reply.at[half, dz], summed.at[half, 4 - dz],
+                rep_s.at[7 * half + 3 + dz], rep_r.at[7 * half + 7 - dz], peer(dz),
+            )
+            for dz in range(1, 4)
+        ]
+        for copy in copies:
+            copy.start()
+        return copies
+
+    def charges_of(half, z_copies):
+        for copy in z_copies:
+            copy.wait_recv()
+        return reply[half, 0] + summed[half, 1] + summed[half, 2] + summed[half, 3]
+
+    y_b, y_a = [], []
     for dy in range(1, 4):
-        lax.fori_loop(4 * dy, 4 * dy + 4, serve, 0)
-        y_copies.append(
-            remote(reply.at[pl.ds(4 * dy, 4)], answer.at[4 - dy], rep_s.at[dy], rep_r.at[4 - dy], peer(4 * dy))
-        )
-        y_copies[-1].start()
+        lax.fori_loop(2 * dy, 2 * dy + 2, serve, 0)
+        y_b.append(send_y(0, dy))
     for k in range(1, 4):
-        remote(ask, asked.at[k], ask_s.at[k], ask_r.at[k], peer(k)).wait_recv()
-        search(k)
-    for copy in y_copies:
-        copy.wait_recv()
-    for k in range(4):
-        reply[k] = reply[k] + answer[1, k] + answer[2, k] + answer[3, k]
-    z_copies = [
-        remote(reply.at[dz], summed.at[4 - dz], rep_s.at[3 + dz], rep_r.at[7 - dz], peer(dz)) for dz in range(1, 4)
-    ]
-    for copy in z_copies:
-        copy.start()
+        asked_by(k)
+    search(0, 0)
+    search(0, 2)
+    for dy in range(1, 3):
+        lax.fori_loop(2 * dy, 2 * dy + 2, serve_a, 0)
+        y_a.append(send_y(1, dy))
+    z_b = send_z(0, y_b)
     for k in range(STRIPS - LATE, STRIPS):
         strip(k)
-    for copy in z_copies:
-        copy.wait_recv()
-    replies = y_copies + z_copies
-    total = reply[0] + summed[1] + summed[2] + summed[3]
-    charge_own[...] = total
+    lax.fori_loop(6, 8, serve_a, 0)
+    y_a.append(send_y(1, 3))
+    lax.fori_loop(0, 2, serve_a, 0)
+    z_a = send_z(1, y_a)
+    replies = y_b + y_a + z_b + z_a
+    total_b = charges_of(0, z_b)
+    charge_own[...] = total_b
     charge_copy = remote(charge_own, charge_got, chg_s, chg_r, dev(n_down, w))
     charge_copy.start()
 
@@ -245,8 +281,9 @@
         mol, a = i // 6, i % 6
         got = []
         for q in range(3):
-            part = charges[6 * q : 6 * q + 6, :]
-            part = jnp.concatenate([part, pltpu.roll(part, 64, 1), jnp.zeros((4, 128), F32)], axis=0)
+            part = charges[3 * q : 3 * q + 3, :]
+            turned = [pltpu.roll(part, 128 - 32 * g, 1) for g in range(1, 4)]
+            part = jnp.concatenate([part, *turned, jnp.zeros((4, 128), F32)], axis=0)
             got.append(jnp.take_along_axis(part, mol + MB * side, axis=1))
         return jnp.where(a < 4, got[0], jnp.where(a == 4, got[1], got[2]))
 
@@ -256,12 +293,12 @@
             one, values, (((0,), (0,)), ((), ())), precision=lax.Precision.HIGHEST, preferred_element_type=F32
         )
 
-    def shifts(f, charges, side, row, col):
-        row_q[f] = pick(row, orbitals(charges, side, lane))
+    def shifts(f, charges, row, col):
+        row_q[f] = pick(row, orbitals(charges, 0, lane))
         for p in range(3):
-            col_q[f, p] = pick(col, orbitals(charges, side + 1, lane + 128 * p))
-
-    shifts(1, total, 2, b_slots[0:1, :], b_slots[1:2, :])
+            col_q[f, p] = pick(col, orbitals(charges, 1, lane + 128 * p))
+
+    shifts(1, total_b, b_slots[0:1, :], b_slots[1:2, :])
 
     wide_lane = iota((SLOTS, 128), 1)
 
@@ -310,7 +347,8 @@
         copy.wait()
     lax.fori_loop(RAW // 4, (RAW + REST) // 4, assemble(1, h_r, m_r, blk_r), 0)
     rest.start()
-    shifts(0, total, 0, a_slots[0:1, :], a_slots[1:2, :])
+    make_r(FULL, 0)
+    shifts(0, charges_of(1, z_a), a_slots[0:1, :], a_slots[1:2, :])
     lax.fori_loop(0, 4, assemble(0, h_l, m_l, blk_l), 0)
 
     @pl.when(core == 0)
@@ -323,7 +361,7 @@
         for k in range(RELAY):
             straight(k).start()
 
-    lax.fori_loop(FULL, CHUNKS, make_r, 0)
+    lax.fori_loop(FULL + 1, CHUNKS, make_r, 0)
     lax.fori_loop(0, RAW // 4, assemble(1, h_r, m_r, blk_r), 0)
     lax.fori_loop(4, 4 * CHUNKS, assemble(0, h_l, m_l, blk_l), 0)
     send_l(1).start()
@@ -411,7 +449,7 @@
     send_l(4).start()
     send_l(5).start()
     charge_copy.wait_recv()
-    shifts(2, charge_got[...], 2, pos_got[1, 1:2, 0:SLOTS], pos_got[1, 2:3, 0:SLOTS])
+    shifts(2, charge_got[...], pos_got[1, 1:2, 0:SLOTS], pos_got[1, 2:3, 0:SLOTS])
     for copy in raws:
         copy.wait_recv()
     lax.fori_loop(0, RAW // 4, assemble(2, raw_h, raw_m, got_r), 0)
@@ -444,7 +482,7 @@
         finish_left(c)
         return 0
 
-    for copy in asks + replies + pos_copies + raws + [tab_copy, charge_copy]:
+    for copy in [all_asks] + replies + pos_copies + raws + [tab_copy, charge_copy]:
         copy.wait_send()
     lax.fori_loop(1, 3, next_left, 0)
     for k in range(RELAY):
@@ -479,8 +517,8 @@
     raw = pltpu.VMEM((SLOTS, RAW * BLK), BF16)
     scratch = [tile] * 8 + [raw] * 2 + [
         pltpu.VMEM((SLOTS, RELAY * PIECE), BF16),
-        pltpu.VMEM((18, 128), F32),
-        pltpu.VMEM((18, 128), F32),
+        pltpu.VMEM((9, 128), F32),
+        pltpu.VMEM((9, 128), F32),
         pltpu.VMEM((2, KPAD, SIDE), BF16),
         pltpu.VMEM((CHUNKS, PART, SIDE), F32),
         pltpu.VMEM((PART, KPAD), BF16),
@@ -491,15 +529,15 @@
         pltpu.VMEM((2, 8, 128), I32),
         pltpu.VMEM((8, 128), I32),
         pltpu.VMEM((CHIPS, 8, 128), I32),
-        pltpu.VMEM((CHIPS, 18, 128), F32),
-        pltpu.VMEM((4, 4, 18, 128), F32),
-        pltpu.VMEM((4, 18, 128), F32),
+        pltpu.VMEM((2, CHIPS, 9, 128), F32),
+        pltpu.VMEM((2, 4, 4, 9, 128), F32),
+        pltpu.VMEM((2, 4, 9, 128), F32),
         pltpu.VMEM((3, HALF, 128), F32),
         pltpu.VMEM((6 * HALF, 256), BF16),
         pltpu.VMEM((3, SLOTS, 128), F32),
         pltpu.VMEM((3, 3, SLOTS, 128), F32),
         dma((4,)),
-        dma((CHIPS,)), dma((CHIPS,)), dma((CHIPS,)), dma((CHIPS,)),
+        dma(()), dma((CHIPS,)), dma((14,)), dma((14,)),
         dma((2,)), dma((2,)), dma(()), dma(()),
         dma((CHUNKS,)), dma((CHUNKS,)), dma((CHUNKS,)), dma((CHUNKS,)),
         dma((2,)), dma((2,)), dma(()), dma(()),

time: 79.2 us -> 77.7 us (0.981)
  Pallas kernels: 75.5 us -> 74.1 us
    pallas_call x1, Pallas kernels: 75.5 us -> 74.1 us  [local(): pl.pallas_call(kernel, out_shape=pltpu.VMEM((TB, BLK, SIDE), BF16), in_sp...]
where the time goes in v2:
time: 77.7 us; the launch traced here: 76.9 us
  Pallas kernels  74.1 us (95%)
  local copies, waits for them, and re-layouts  1.5 us (2%)
  between operations  1.31 us (2%)
    pallas_call x1, Pallas kernels, local(): pl.pallas_call(kernel, out_shape=pltpu.VMEM((TB, BLK, SIDE), BF16), in_sp...  74.1 us

profile of v2, /device:TPU:53, one launch (start us, length us, event | category | flops | bytes accessed | tf_op | source)
XLA Modules:
  0.0 76.9 jit_solution(9265479823565327238)
XLA Ops:
  1.3 74.1 %shard_map.109 = bf16[12,96,1152]{2,1,0:T(8,128)(2,1)S(1)} custom-call(bf16[72,9216]{1,0:T(8,128)(2,1)} %bitcast.14, bf16[72,9216]{1,0:T(8,128)(2,1)} %bitcast.15, s32[2,72]{1,0:T(2,128)} %bitcast.20, s32[1,1]{1,0:T(1,128)S(6)} %copy.14.a_count, s32[12,2,16]{2,1,0:T(2,128)} %bitcast.18, bf16[72,9216]{1,0:T(8,128)(2,1)} %bitcast.16, ...), custom_call_target="tpu_custom_call" | custom-call | flops 14000000000 | bytes 9000000 | tf_op jit(solution)/shard_map/pallas_call | solution.py:546
  75.4 1.5 %copy.13 = bf16[1,1,1152,1152]{3,2,1,0:T(8,128)(2,1)} copy(bf16[1,1,1152,1152]{3,2,1,0:T(8,128)(2,1)S(1)} %bitcast.13) | data formatting | bytes 5308416
